TPU v7x, 32 devices: a whole 2x2x4 slice. The times are simulated.
32 devices in a mesh: row: 4 (over y, x), col: 8 (over z, core).
Axes of the slice: x: 2, y: 2, z: 4, core: 2. Of those that a mesh axis runs over, the one named last changes fastest.
Arguments:
- filtered_bands: bfloat16 [4096, 16384], P(None, ('row', 'col')), may hold values from -0.09375 to 0.09375
Outputs:
- gram_upper: float32 [16384, 16384], P('row', 'col')
All inputs are finite; a program needn't handle non-finite values.
Results may differ from a plain program's by a relative error of at most 0.0003.
Values may be sent and summed in bfloat16 or wider, within the bound.
A program may use at most 192 MiB of HBM per device.

v0:
```python
import jax
import jax.numpy as jnp
from jax import lax
from jax.sharding import PartitionSpec as P


def from_root(shard, axis, root):
    mine = lax.axis_index(axis) == root
    return lax.psum(jnp.where(mine, shard, jnp.zeros_like(shard)), axis)


def tile_product(left_panel, right_panel):
    return lax.dot_general(
        left_panel, right_panel, (((0,), (0,)), ((), ())), preferred_element_type=jnp.float32
    )


def shards(filtered_bands):
    row_count = lax.axis_size("row")
    col_count = lax.axis_size("col")
    own_bands = filtered_bands.shape[1]
    tile_rows = own_bands * col_count
    tile_cols = own_bands * row_count
    grid_ratio = col_count // row_count
    row_index = lax.axis_index("row")
    col_index = lax.axis_index("col")
    half_rows = filtered_bands.shape[0] // 2
    below_diag = (col_index + 1) * tile_cols <= row_index * tile_rows
    accumulated = jnp.zeros((tile_rows, tile_cols), jnp.float32)
    for summa_step in range(2):
        own_part = filtered_bands[summa_step * half_rows : (summa_step + 1) * half_rows]
        left_panel = lax.all_gather(own_part, "col", axis=1, tiled=True)
        column_piece = lax.dynamic_slice_in_dim(
            left_panel, col_index % grid_ratio * tile_cols, tile_cols, 1
        )
        right_panel = from_root(column_piece, "row", col_index // grid_ratio)
        accumulated = lax.cond(
            below_diag,
            lambda current, lhs, rhs: current,
            lambda current, lhs, rhs: current + tile_product(lhs, rhs),
            accumulated,
            left_panel,
            right_panel,
        )
    global_rows = row_index * tile_rows + lax.broadcasted_iota(jnp.int32, (tile_rows, tile_cols), 0)
    global_cols = col_index * tile_cols + lax.broadcasted_iota(jnp.int32, (tile_rows, tile_cols), 1)
    return jnp.where(global_cols >= global_rows, accumulated, jnp.float32(0.0))


def solution(mesh):
    return jax.shard_map(
        shards,
        mesh=mesh,
        in_specs=(P(None, ("row", "col")),),
        out_specs=P("row", "col"),
        check_vma=False,
    )
```

profile of v0, /device:TPU:0, one launch (start us, length us, event | category | flops | bytes accessed | tf_op | source)
XLA Modules:
  0.0 752.2 jit_solution(3805099503593361425)
XLA Ops:
  6.5 0.0 all-gather.3.cloned.1.call-start
  6.5 4.5 fusion
  11.0 0.0 all-gather.3.cloned.1.call-update
  11.1 0.0 all-gather.5.cloned.1.call-start
  11.1 0.7 all-gather.5.cloned.1.call-update
  11.8 0.0 all-reduce.3.cloned.1.call-start
  11.9 153.1 %all-gather.3.cloned.1.call-done = bf16[2048,4096]{1,0:T(8,128)(2,1)} async-done(((bf16[2048,512]{1,0:T(8,128)(2,1)}), bf16[2048,4096]{1,0:T(8,128)(2,1)}) %all-gather.3.cloned.1.call-update) | async-done | bytes 16777232 | tf_op jit(solution)/shard_map/all_gather | solution.py:32
  165.0 10.5 %dynamic-slice_select_fusion.1 = bf16[2048,2048]{1,0:T(8,128)(2,1)} fusion(bf16[2048,4096]{1,0:T(8,128)(2,1)} %all-gather.3.cloned.1.call-done, s32[]{:T(128)S(6)} %select_n.37, pred[]{:T(512)S(6)} %eq.7), kind=kLoop, calls=%fused_computation.3 | loop fusion | flops 4194304 | bytes 16777220 | tf_op jit(solution)/shard_map/jit(_where)/select_n | solution.py:9
  175.5 140.4 %all-gather.5.cloned.1.call-done = bf16[2048,4096]{1,0:T(8,128)(2,1)} async-done(((bf16[2048,512]{1,0:T(8,128)(2,1)}), bf16[2048,4096]{1,0:T(8,128)(2,1)}) %all-gather.5.cloned.1.call-update) | async-done | bytes 16777232 | tf_op jit(solution)/shard_map/all_gather | solution.py:32
  316.0 9.7 %dynamic-slice_select_fusion = bf16[2048,2048]{1,0:T(8,128)(2,1)} fusion(bf16[2048,4096]{1,0:T(8,128)(2,1)} %all-gather.5.cloned.1.call-done, s32[]{:T(128)S(6)} %select_n.37, pred[]{:T(512)S(6)} %eq.7), kind=kLoop, calls=%fused_computation.2 | loop fusion | flops 4194304 | bytes 16777220 | tf_op jit(solution)/shard_map/jit(_where)/select_n | solution.py:9
  325.6 0.0 all-reduce.3.cloned.1.call-update
  325.7 306.6 %all-reduce.3.cloned.1.call-done = (bf16[2048,2048]{1,0:T(8,128)(2,1)}, bf16[2048,2048]{1,0:T(8,128)(2,1)}) async-done(((bf16[2048,2048]{1,0:T(8,128)(2,1)}, bf16[2048,2048]{1,0:T(8,128)(2,1)}), (bf16[2048,2048]{1,0:T(8,128)(2,1)}, bf16[2048,2048]{1,0:T(8,128)(2,1)})) %all-reduce.3.cloned.1.call-update) | async-done | bytes 16777232 | tf_op jit(solution)/shard_map/psum | solution.py:9
  632.2 43.9 %conditional.2 = (f32[4096,2048]{1,0:T(8,128)}) conditional(s32[]{:T(128)} %convert_element_type.4, (bf16[2048,4096]{1,0:T(8,128)(2,1)}, bf16[2048,2048]{1,0:T(8,128)(2,1)}) %tuple.17, () %tuple.18), branch_computations={%region_2.3_spmd, %region_3.4_spmd} | conditional | flops 34359738368 | bytes 58720264 | solution.py:37
  632.2 43.9 %fusion.1 = f32[4096,2048]{1,0:T(8,128)} fusion(bf16[2048,4096]{1,0:T(8,128)(2,1)} %get-tuple-element.22, bf16[2048,2048]{1,0:T(8,128)(2,1)} %get-tuple-element.23), kind=kOutput, calls=%fused_computation.7 | convolution fusion | flops 34359738368 | bytes 58720256 | tf_op jit(solution)/shard_map/cond/branch_0_fun/dot_general | solution.py:13
  676.1 46.3 %conditional.3 = (f32[4096,2048]{1,0:T(8,128)}) conditional(s32[]{:T(128)} %convert_element_type.4, (bf16[2048,4096]{1,0:T(8,128)(2,1)}, bf16[2048,2048]{1,0:T(8,128)(2,1)}, f32[4096,2048]{1,0:T(8,128)}) %tuple.19, f32[4096,2048]{1,0:T(8,128)} %get-tuple-element.33), branch_computations={%region_4.5_spmd, %region_5.6_spmd} | conditional | flops 34368126976 | bytes 92274696 | solution.py:37
  676.1 46.3 %convolution_add_fusion = f32[4096,2048]{1,0:T(8,128)} fusion(f32[4096,2048]{1,0:T(8,128)} %get-tuple-element.24, bf16[2048,4096]{1,0:T(8,128)(2,1)} %get-tuple-element.25, bf16[2048,2048]{1,0:T(8,128)(2,1)} %get-tuple-element.26), kind=kOutput, calls=%fused_computation | convolution fusion | flops 34368126976 | bytes 92274688 | tf_op jit(solution)/shard_map/cond/branch_0_fun/dot_general | solution.py:13
  722.5 23.2 %compare_select_fusion = f32[4096,2048]{1,0:T(8,128)} fusion(f32[4096,2048]{1,0:T(8,128)} %get-tuple-element.34, s32[2048]{0:T(1024)S(1)} %iota_add_fusion.1, s32[4096]{0:T(1024)S(1)} %iota_add_fusion), kind=kLoop, calls=%fused_computation.1 | loop fusion | flops 16777216 | bytes 67133440 | tf_op jit(solution)/shard_map/jit(_where)/select_n | solution.py:47
  (2 shorter events, 0.0 us)
Async XLA Ops:
  6.5 158.5 %all-gather.3.cloned.1.call-start = ((), (), s32[]{:S(2)}) async-start(), calls=%async_computation | async-start | bytes 18874368 | tf_op jit(solution)/shard_map/all_gather | solution.py:32
  11.1 304.9 %all-gather.5.cloned.1.call-start = ((), (), s32[]{:S(2)}) async-start(), calls=%async_computation.1 | async-start | bytes 18874368 | tf_op jit(solution)/shard_map/all_gather | solution.py:32
  11.8 620.4 %all-reduce.3.cloned.1.call-start = ((), (), s32[]{:S(2)}) async-start(), calls=%async_computation.2 | async-start | bytes 33554432 | tf_op jit(solution)/shard_map/psum | solution.py:9
Sparse Core Ops, SparseCore 0:
  11.2 153.7 all-gather.2
  166.6 149.2 all-gather.4
  325.8 306.4 all-reduce.2
where the time goes:
time: 753 us; the launch traced here: 752 us
  waiting for transfers between devices  601 us (80%)
  matrix products  90.2 us (12%)
  other arithmetic  43.4 us (6%)
  between operations  13.2 us (2%)
    psum x1, waiting for transfers between devices, from_root(): return lax.psum(jnp.where(mine, shard, jnp.zeros_like(shard)), axis)  307 us
    all_gather x2, waiting for transfers between devices, shards(): left_panel = lax.all_gather(own_part, 'col', axis=1, tiled=True)  294 us
    dot_general x2, matrix products, tile_product(): lax.dot_general(left_panel, right_panel, (((0,), (0,)), ((), ())), prefer...  90.2 us
    select_n x1, other arithmetic, shards(): return jnp.where(global_cols >= global_rows, accumulated, jnp.float32(0.0))  23.2 us
    select_n x2, other arithmetic, from_root(): return lax.psum(jnp.where(mine, shard, jnp.zeros_like(shard)), axis)  20.2 us
  transfers between devices with their start and end apart: 3, of which 3 were waited for; matrix products, arithmetic and copies ran while one was open for 1% of the time, Pallas kernels for 0%

commit v1 on v0

v1 whole, which is shorter than its diff:
```python
import functools

import jax
import jax.numpy as jnp
from jax import lax
from jax.experimental import pallas as pl
from jax.experimental.pallas import tpu as pltpu
from jax.sharding import PartitionSpec as P

MESH = pl.DeviceIdType.MESH
CHUNKS = 8
AHEAD = 2
VMEM_BYTES = 56 * 2**20


def ring_place(row, count):
    return jnp.where(row % 2 == 0, row // 2, count - 1 - row // 2)


def ring_row(place, count):
    return jnp.where(place < count // 2, 2 * place, 2 * (count - 1 - place) + 1)


def hops_needed(count, group, direction):
    place = lambda row: row // 2 if row % 2 == 0 else count - 1 - row // 2
    steps = [(direction * (place(row) - place(group))) % count for row in range(group)]
    return max(steps, default=0)


def gather_kernel(
    row_count, col_count, own_ref, rows_ref, cols_ref, part_ref,
    rows_v, cols_v, total,
    row_recv, sib_recv, col_recv, up_send, down_send, sib_send, col_send, local, load,
):
    chips = col_count // 2
    depth, bands = own_ref.shape
    piece = depth // CHUNKS
    row = lax.axis_index("row")
    col = lax.axis_index("col")
    chip, core = col // 2, col % 2
    wanted = chip >= row
    diagonal = chip == row

    upper = (row, col + 2)
    lower = (row, col - 2)
    sibling = (row, chip * 2 + 1 - core)
    forward = core == 0
    here, start = ring_place(row, row_count), ring_place(chip, row_count)
    after, before = (here + 1) % row_count, (here + row_count - 1) % row_count
    row_after, row_before = ring_row(after, row_count), ring_row(before, row_count)
    hop = jnp.where(
        forward, (here - start + row_count) % row_count, (start - here + row_count) % row_count
    )
    hops = jnp.int32(0)
    for group in range(row_count):
        fixed = jnp.where(
            forward, hops_needed(row_count, group, 1), hops_needed(row_count, group, -1)
        )
        hops = jnp.where(chip == group, fixed, hops)
    next_on_ring = (jnp.where(forward, row_after, row_before), col)
    takes_cols = (hop >= 1) & (hop <= hops)
    gives_cols = hop < hops

    barrier = pltpu.get_barrier_semaphore()

    def greet(device):
        pl.semaphore_signal(barrier, inc=1, device_id=device, device_id_type=MESH)

    has_upper, has_lower = chip < chips - 1, chip > 0
    pl.when(has_upper)(lambda: greet(upper))
    pl.when(has_lower)(lambda: greet(lower))
    greet(sibling)
    greet((row_after, col))
    greet((row_before, col))
    pl.semaphore_wait(barrier, 3 + has_upper.astype(jnp.int32) + has_lower.astype(jnp.int32))

    def part(j):
        return pl.ds(pl.multiple_of(j * piece, piece), piece)

    def block_copy(source, chip_at, j, send, recv, device):
        block = chip_at * 2 + core
        return pltpu.make_async_remote_copy(
            src_ref=own_ref.at[part(j)] if source == "own" else rows_ref.at[block, part(j)],
            dst_ref=rows_ref.at[block, part(j)],
            send_sem=send.at[chip_at, j],
            recv_sem=recv.at[chip_at, j],
            device_id=device,
            device_id_type=MESH,
        )

    def up(source, chip_at, j):
        return block_copy(source, chip_at, j, up_send, row_recv, upper)

    def down(source, chip_at, j):
        return block_copy(source, chip_at, j, down_send, row_recv, lower)

    def across(source, chip_at, j):
        return block_copy(source, chip_at, j, sib_send, sib_recv, sibling)

    def col_copy(from_rows, i, j):
        return pltpu.make_async_remote_copy(
            src_ref=rows_ref.at[core * row_count + i, part(j)]
            if from_rows
            else cols_ref.at[i, part(j)],
            dst_ref=cols_ref.at[i, part(j)],
            send_sem=col_send.at[i, j],
            recv_sem=col_recv.at[i, j],
            device_id=next_on_ring,
            device_id_type=MESH,
        )

    sends_down = has_lower & (chip - 1 >= row)

    def send_own(j):
        pl.when(has_upper)(lambda: up("own", chip, j).start())
        pl.when(sends_down)(lambda: down("own", chip, j).start())
        pl.when(wanted)(lambda: across("own", chip, j).start())

    for j in range(AHEAD):
        send_own(j)
    own_copy = pltpu.make_async_copy(own_ref, rows_ref.at[col], local.at[0])
    own_copy.start()

    @pl.when(wanted)
    def _():
        @pl.loop(0, total.shape[0] // bands)
        def _(rb):
            at = pl.ds(pl.multiple_of(rb * bands, bands), bands)
            total[at, :] = jnp.zeros((bands, total.shape[1]), jnp.float32)

    own_copy.wait()

    def multiply(j):
        rows_load = pltpu.make_async_copy(rows_ref.at[:, part(j)], rows_v, load.at[0])
        cols_load = pltpu.make_async_copy(cols_ref.at[:, part(j)], cols_v, load.at[1])
        rows_load.start()
        cols_load.start()
        rows_load.wait()
        cols_load.wait()

        @pl.loop(0, col_count)
        def _(rb):
            lhs = rows_v[rb].T
            at = pl.ds(pl.multiple_of(rb * bands, bands), bands)
            for cb in range(row_count):

                @pl.when(jnp.logical_not(diagonal) | (core * row_count + cb >= rb))
                def _():
                    there = pl.ds(cb * bands, bands)
                    total[at, there] += jnp.dot(
                        lhs, cols_v[cb], preferred_element_type=jnp.float32
                    )

    def save():
        return pltpu.make_async_copy(total, part_ref, load.at[2])

    @pl.loop(0, CHUNKS)
    def _(j):
        pl.when(j + AHEAD < CHUNKS)(lambda: send_own(j + AHEAD))
        for d in range(1, chips):

            @pl.when(chip >= d)
            def _():
                at = chip - d
                up("rows", at, j).wait_recv()
                pl.when(has_upper)(lambda: up("rows", at, j).start())
                pl.when(wanted)(lambda: across("rows", at, j).start())

        for d in range(1, chips):

            @pl.when(wanted & (chip + d < chips))
            def _():
                at = chip + d
                down("rows", at, j).wait_recv()
                pl.when(sends_down)(lambda: down("rows", at, j).start())
                across("rows", at, j).start()

        @pl.when(takes_cols)
        def _():
            for i in range(row_count):
                col_copy(False, i, j).wait_recv()
                pl.when(gives_cols)(lambda: col_copy(False, i, j).start())

        @pl.when(wanted)
        def _():
            for at in range(chips):
                other = at * 2 + 1 - core
                pltpu.make_async_remote_copy(
                    src_ref=rows_ref.at[other, part(j)],
                    dst_ref=rows_ref.at[other, part(j)],
                    send_sem=sib_send.at[at, j],
                    recv_sem=sib_recv.at[at, j],
                    device_id=sibling,
                    device_id_type=MESH,
                ).wait_recv()

        @pl.when(diagonal)
        def _():
            for i in range(row_count):
                pl.when(gives_cols)(lambda: col_copy(True, i, j).start())
            mine = pltpu.make_async_copy(
                rows_ref.at[pl.ds(core * row_count, row_count), part(j)],
                cols_ref.at[:, part(j)],
                local.at[1],
            )
            mine.start()
            mine.wait()

        @pl.when(wanted & (j < CHUNKS - 1))
        def _():
            multiply(j)
            pl.when(j == CHUNKS - 2)(lambda: save().start())

    @pl.loop(0, CHUNKS)
    def _(j):
        for at in range(chips):
            pl.when(has_upper & (chip >= at))(lambda: up("rows", at, j).wait_send())
            pl.when(sends_down & (chip <= at))(lambda: down("rows", at, j).wait_send())
            pl.when(wanted)(lambda: across("rows", at, j).wait_send())
        for i in range(row_count):
            pl.when(gives_cols)(lambda: col_copy(False, i, j).wait_send())

    pl.when(wanted)(lambda: save().wait())


def finish_kernel(rows_ref, cols_ref, part_ref, out_ref):
    bands = rows_ref.shape[2]
    tile_cols = out_ref.shape[1]
    row = lax.axis_index("row")
    col = lax.axis_index("col")
    rb = pl.program_id(0)
    first_row = (row * pl.num_programs(0) + rb) * bands
    first_col = col * tile_cols
    needed = first_col + tile_cols > first_row

    @pl.when(needed)
    def _():
        lhs = rows_ref[0].T
        for cb in range(tile_cols // bands):
            at = pl.ds(cb * bands, bands)
            value = part_ref[:, at] + jnp.dot(
                lhs, cols_ref[cb], preferred_element_type=jnp.float32
            )
            global_rows = first_row + lax.broadcasted_iota(jnp.int32, (bands, bands), 0)
            global_cols = (
                first_col + cb * bands + lax.broadcasted_iota(jnp.int32, (bands, bands), 1)
            )
            out_ref[:, at] = jnp.where(global_cols >= global_rows, value, 0.0)

    @pl.when(jnp.logical_not(needed))
    def _():
        out_ref[...] = jnp.zeros_like(out_ref)


def shards(row_count, col_count, own):
    depth, bands = own.shape
    tile_rows, tile_cols = bands * col_count, bands * row_count
    piece = depth // CHUNKS
    chips = col_count // 2
    hbm = pl.BlockSpec(memory_space=pl.ANY)
    flops = 2 * tile_rows * tile_cols * depth
    dma = lambda first: pltpu.SemaphoreType.DMA((first, CHUNKS))
    rows, cols, part = pl.pallas_call(
        functools.partial(gather_kernel, row_count, col_count),
        out_shape=(
            jax.ShapeDtypeStruct((col_count, depth, bands), own.dtype),
            jax.ShapeDtypeStruct((row_count, depth, bands), own.dtype),
            jax.ShapeDtypeStruct((tile_rows, tile_cols), jnp.float32),
        ),
        in_specs=[hbm],
        out_specs=(hbm, hbm, hbm),
        scratch_shapes=[
            pltpu.VMEM((col_count, piece, bands), own.dtype),
            pltpu.VMEM((row_count, piece, bands), own.dtype),
            pltpu.VMEM((tile_rows, tile_cols), jnp.float32),
            dma(chips), dma(chips), dma(row_count),
            dma(chips), dma(chips), dma(chips), dma(row_count),
            pltpu.SemaphoreType.DMA((2,)),
            pltpu.SemaphoreType.DMA((3,)),
        ],
        compiler_params=pltpu.CompilerParams(
            collective_id=0, has_side_effects=True, vmem_limit_bytes=VMEM_BYTES
        ),
        cost_estimate=pl.CostEstimate(
            flops=flops * (CHUNKS - 1) // CHUNKS,
            bytes_accessed=(tile_rows + tile_cols) * (2 * depth + 2 * tile_cols),
            transcendentals=0,
        ),
        name="gather",
    )(own)
    return pl.pallas_call(
        finish_kernel,
        grid=(col_count,),
        out_shape=jax.ShapeDtypeStruct((tile_rows, tile_cols), jnp.float32),
        in_specs=[
            pl.BlockSpec((1, piece, bands), lambda rb: (rb, CHUNKS - 1, 0)),
            pl.BlockSpec((row_count, piece, bands), lambda rb: (0, CHUNKS - 1, 0)),
            pl.BlockSpec((bands, tile_cols), lambda rb: (rb, 0)),
        ],
        out_specs=pl.BlockSpec((bands, tile_cols), lambda rb: (rb, 0)),
        compiler_params=pltpu.CompilerParams(vmem_limit_bytes=VMEM_BYTES),
        cost_estimate=pl.CostEstimate(
            flops=flops // CHUNKS,
            bytes_accessed=8 * tile_rows * tile_cols,
            transcendentals=0,
        ),
        name="finish",
    )(rows, cols, part)


def solution(mesh):
    return jax.shard_map(
        functools.partial(shards, mesh.shape["row"], mesh.shape["col"]),
        mesh=mesh,
        in_specs=(P(None, ("row", "col")),),
        out_specs=P("row", "col"),
        check_vma=False,
    )
```

time: 753 us -> 1000 us (1.33); the launches traced: 752 us -> 989 us
  Pallas kernels: 0 us -> 989 us
  waiting for transfers between devices: 601 us -> 0 us
  matrix products: 90.2 us -> 0 us
  other arithmetic: 43.4 us -> 0 us
  between operations: 13.2 us -> 0.01 us
    pallas_call x0 -> x2, Pallas kernels: none -> 989 us  [the longest x1 963 us: shards(): pl.pallas_call(functools.partial(gather_kernel, row_count, col_count), ou...]
    psum x1 -> x0, waiting for transfers between devices: 307 us -> none  [from_root(): return lax.psum(jnp.where(mine, shard, jnp.zeros_like(shard)), axis)]
    all_gather x2 -> x0, waiting for transfers between devices: 294 us -> none  [shards(): left_panel = lax.all_gather(own_part, 'col', axis=1, tiled=True)]
    dot_general x2 -> x0, matrix products: 90.2 us -> none  [tile_product(): lax.dot_general(left_panel, right_panel, (((0,), (0,)), ((), ())), prefer...]
    select_n x3 -> x0, other arithmetic: 43.4 us -> none  [the longest x1 23.2 us: shards(): return jnp.where(global_cols >= global_rows, accumulated, jnp.float32(0.0))]
  transfers between devices with their start and end apart: 3 -> 0, of which waited for: 3 -> 0; matrix products, arithmetic and copies ran while one was open for 1% -> 0% of each run, Pallas kernels for 0% -> 0%
where the time goes in v1:
time: 1000 us; the launch traced here: 989 us
  Pallas kernels  989 us (99%)
    pallas_call x1, Pallas kernels, shards(): pl.pallas_call(functools.partial(gather_kernel, row_count, col_count), ou...  963 us
    pallas_call x1, Pallas kernels, shards(): pl.pallas_call(finish_kernel, grid=(col_count,), out_shape=jax.ShapeDtype...  25.7 us

profile of v1, /device:TPU:0, one launch (start us, length us, event | category | flops | bytes accessed | tf_op | source)
XLA Modules:
  0.0 988.7 jit_solution(7963382244952830785)
XLA Ops:
  0.0 963.0 %gather.1 = (bf16[8,4096,512]{2,1,0:T(8,128)(2,1)}, bf16[4,4096,512]{2,1,0:T(8,128)(2,1)}, f32[4096,2048]{1,0:T(8,128)}) custom-call(bf16[4096,512]{1,0:T(8,128)(2,1)} %own_ref.1), custom_call_target="tpu_custom_call" | custom-call | flops 60129542144 | bytes 75497472 | tf_op jit(solution)/shard_map/gather/pallas_call | solution.py:263
  963.0 25.7 %finish.1 = f32[4096,2048]{1,0:T(8,128)} custom-call(bf16[8,4096,512]{2,1,0:T(8,128)(2,1)} %get-tuple-element.8.rows_ref, bf16[4,4096,512]{2,1,0:T(8,128)(2,1)} %get-tuple-element.9.cols_ref, f32[4096,2048]{1,0:T(8,128)} %get-tuple-element.10.part_ref), custom_call_target="tpu_custom_call" | custom-call | flops 8589934592 | bytes 67108864 | tf_op jit(solution)/shard_map/finish/pallas_call | solution.py:291

commit v2 on v1

--- a/solution.py
+++ b/solution.py
@@ -9,7 +9,7 @@
 
 MESH = pl.DeviceIdType.MESH
 CHUNKS = 8
-AHEAD = 2
+AHEAD = 1
 VMEM_BYTES = 56 * 2**20
 
 
@@ -30,7 +30,7 @@
 def gather_kernel(
     row_count, col_count, own_ref, rows_ref, cols_ref, part_ref,
     rows_v, cols_v, total,
-    row_recv, sib_recv, col_recv, up_send, down_send, sib_send, col_send, local, load,
+    row_recv, sib_recv, col_recv, up_send, down_send, sib_send, col_send, local, load, saved,
 ):
     chips = col_count // 2
     depth, bands = own_ref.shape
@@ -118,29 +118,57 @@
 
     for j in range(AHEAD):
         send_own(j)
-    own_copy = pltpu.make_async_copy(own_ref, rows_ref.at[col], local.at[0])
-    own_copy.start()
+
+    def own_in(j):
+        return pltpu.make_async_copy(
+            own_ref.at[part(j)], rows_v.at[0, j % col_count], local.at[0, j]
+        )
+
+    def own_out(j):
+        return pltpu.make_async_copy(
+            rows_v.at[0, j % col_count], rows_ref.at[col, part(j)], local.at[1, j]
+        )
 
     @pl.when(wanted)
     def _():
+        for first in range(0, CHUNKS, col_count):
+            batch = range(first, min(first + col_count, CHUNKS))
+            for j in batch:
+                own_in(j).start()
+            for j in batch:
+                own_in(j).wait()
+                own_out(j).start()
+            for j in batch:
+                own_out(j).wait()
+
         @pl.loop(0, total.shape[0] // bands)
         def _(rb):
             at = pl.ds(pl.multiple_of(rb * bands, bands), bands)
             total[at, :] = jnp.zeros((bands, total.shape[1]), jnp.float32)
 
-    own_copy.wait()
+    same_rows = pl.ds(core * row_count, row_count)
+
+    def load_rows(j):
+        return pltpu.make_async_copy(
+            rows_ref.at[:, part(j)], rows_v.at[j % 2], load.at[0, j % 2]
+        )
+
+    def load_cols(j, same):
+        source = rows_ref.at[same_rows, part(j)] if same else cols_ref.at[:, part(j)]
+        return pltpu.make_async_copy(source, cols_v.at[j % 2], load.at[1, j % 2])
+
+    def fetch(j):
+        load_rows(j).start()
+        pl.when(diagonal)(lambda: load_cols(j, True).start())
+        pl.when(jnp.logical_not(diagonal))(lambda: load_cols(j, False).start())
 
     def multiply(j):
-        rows_load = pltpu.make_async_copy(rows_ref.at[:, part(j)], rows_v, load.at[0])
-        cols_load = pltpu.make_async_copy(cols_ref.at[:, part(j)], cols_v, load.at[1])
-        rows_load.start()
-        cols_load.start()
-        rows_load.wait()
-        cols_load.wait()
+        load_rows(j).wait()
+        load_cols(j, False).wait()
 
         @pl.loop(0, col_count)
         def _(rb):
-            lhs = rows_v[rb].T
+            lhs = rows_v[j % 2, rb].T
             at = pl.ds(pl.multiple_of(rb * bands, bands), bands)
             for cb in range(row_count):
 
@@ -148,14 +176,25 @@
                 def _():
                     there = pl.ds(cb * bands, bands)
                     total[at, there] += jnp.dot(
-                        lhs, cols_v[cb], preferred_element_type=jnp.float32
+                        lhs, cols_v[j % 2, cb], preferred_element_type=jnp.float32
                     )
 
     def save():
-        return pltpu.make_async_copy(total, part_ref, load.at[2])
-
-    @pl.loop(0, CHUNKS)
-    def _(j):
+        return pltpu.make_async_copy(total, part_ref, saved)
+
+    def sibling_arrived(j):
+        for at in range(chips):
+            other = at * 2 + 1 - core
+            pltpu.make_async_remote_copy(
+                src_ref=rows_ref.at[other, part(j)],
+                dst_ref=rows_ref.at[other, part(j)],
+                send_sem=sib_send.at[at, j],
+                recv_sem=sib_recv.at[at, j],
+                device_id=sibling,
+                device_id_type=MESH,
+            ).wait_recv()
+
+    def pass_rows(j):
         pl.when(j + AHEAD < CHUNKS)(lambda: send_own(j + AHEAD))
         for d in range(1, chips):
 
@@ -175,41 +214,52 @@
                 pl.when(sends_down)(lambda: down("rows", at, j).start())
                 across("rows", at, j).start()
 
+        @pl.when(diagonal)
+        def _():
+            sibling_arrived(j)
+            for i in range(row_count):
+                pl.when(gives_cols)(lambda: col_copy(True, i, j).start())
+
+    def pass_cols(j):
         @pl.when(takes_cols)
         def _():
             for i in range(row_count):
                 col_copy(False, i, j).wait_recv()
                 pl.when(gives_cols)(lambda: col_copy(False, i, j).start())
 
-        @pl.when(wanted)
+    @pl.loop(0, CHUNKS)
+    def _(j):
+        pass_rows(j)
+
+        @pl.when(j >= 1)
         def _():
-            for at in range(chips):
-                other = at * 2 + 1 - core
-                pltpu.make_async_remote_copy(
-                    src_ref=rows_ref.at[other, part(j)],
-                    dst_ref=rows_ref.at[other, part(j)],
-                    send_sem=sib_send.at[at, j],
-                    recv_sem=sib_recv.at[at, j],
-                    device_id=sibling,
-                    device_id_type=MESH,
-                ).wait_recv()
-
-        @pl.when(diagonal)
-        def _():
-            for i in range(row_count):
-                pl.when(gives_cols)(lambda: col_copy(True, i, j).start())
-            mine = pltpu.make_async_copy(
-                rows_ref.at[pl.ds(core * row_count, row_count), part(j)],
-                cols_ref.at[:, part(j)],
-                local.at[1],
-            )
-            mine.start()
-            mine.wait()
-
-        @pl.when(wanted & (j < CHUNKS - 1))
-        def _():
-            multiply(j)
-            pl.when(j == CHUNKS - 2)(lambda: save().start())
+            pass_cols(j - 1)
+            pl.when(wanted & jnp.logical_not(diagonal))(lambda: sibling_arrived(j - 1))
+
+            @pl.when(wanted)
+            def _():
+                fetch(j - 1)
+                pl.when(j >= 2)(lambda: multiply(j - 2))
+
+    pl.when(gives_cols)(lambda: pass_cols(CHUNKS - 1))
+
+    @pl.when(wanted)
+    def _():
+        multiply(CHUNKS - 2)
+        save().start()
+
+    pl.when(jnp.logical_not(gives_cols))(lambda: pass_cols(CHUNKS - 1))
+    pl.when(wanted & jnp.logical_not(diagonal))(lambda: sibling_arrived(CHUNKS - 1))
+
+    @pl.when(diagonal)
+    def _():
+        load_cols(CHUNKS - 1, True).start()
+        load_cols(CHUNKS - 1, True).wait()
+        mine = pltpu.make_async_copy(
+            cols_v.at[(CHUNKS - 1) % 2], cols_ref.at[:, part(CHUNKS - 1)], load.at[1, 0]
+        )
+        mine.start()
+        mine.wait()
 
     @pl.loop(0, CHUNKS)
     def _(j):
@@ -270,13 +320,14 @@
         in_specs=[hbm],
         out_specs=(hbm, hbm, hbm),
         scratch_shapes=[
-            pltpu.VMEM((col_count, piece, bands), own.dtype),
-            pltpu.VMEM((row_count, piece, bands), own.dtype),
+            pltpu.VMEM((2, col_count, piece, bands), own.dtype),
+            pltpu.VMEM((2, row_count, piece, bands), own.dtype),
             pltpu.VMEM((tile_rows, tile_cols), jnp.float32),
             dma(chips), dma(chips), dma(row_count),
             dma(chips), dma(chips), dma(chips), dma(row_count),
-            pltpu.SemaphoreType.DMA((2,)),
-            pltpu.SemaphoreType.DMA((3,)),
+            dma(2),
+            pltpu.SemaphoreType.DMA((2, 2)),
+            pltpu.SemaphoreType.DMA,
         ],
         compiler_params=pltpu.CompilerParams(
             collective_id=0, has_side_effects=True, vmem_limit_bytes=VMEM_BYTES

time: 1000 us -> 450 us (0.45)
  the two profiles are of different devices: /device:TPU:0 before, /device:TPU:28 now
where the time goes in v2:
time: 450 us
  Pallas kernels  450 us (100%)
    pallas_call x1, Pallas kernels, shards(): pl.pallas_call(functools.partial(gather_kernel, row_count, col_count), ou...  422 us
    pallas_call x1, Pallas kernels, shards(): pl.pallas_call(finish_kernel, grid=(col_count,), out_shape=jax.ShapeDtype...  27.5 us

profile of v2, /device:TPU:28, one launch (start us, length us, event | category | flops | bytes accessed | tf_op | source)
XLA Modules:
  0.0 449.9 jit_solution(16716523212646954058)
XLA Ops:
  0.0 422.4 %gather.1 = (bf16[8,4096,512]{2,1,0:T(8,128)(2,1)}, bf16[4,4096,512]{2,1,0:T(8,128)(2,1)}, f32[4096,2048]{1,0:T(8,128)}) custom-call(bf16[4096,512]{1,0:T(8,128)(2,1)} %own_ref.1), custom_call_target="tpu_custom_call" | custom-call | flops 60129542144 | bytes 75497472 | tf_op jit(solution)/shard_map/gather/pallas_call | solution.py:313
  422.4 27.5 %finish.1 = f32[4096,2048]{1,0:T(8,128)} custom-call(bf16[8,4096,512]{2,1,0:T(8,128)(2,1)} %get-tuple-element.8.rows_ref, bf16[4,4096,512]{2,1,0:T(8,128)(2,1)} %get-tuple-element.9.cols_ref, f32[4096,2048]{1,0:T(8,128)} %get-tuple-element.10.part_ref), custom_call_target="tpu_custom_call" | custom-call | flops 8589934592 | bytes 67108864 | tf_op jit(solution)/shard_map/finish/pallas_call | solution.py:342
